TPU v7x, 32 devices: a whole 2x2x4 slice. The times are simulated.
32 devices in a mesh: seg: 32 (over z, y, x, core).
Axes of the slice: x: 2, y: 2, z: 4, core: 2. Of those that a mesh axis runs over, the one named last changes fastest.
Arguments:
- density: float32 [2, 12288, 256], P(None, 'seg'), may hold values from -6 to 6
- near_blocks: bfloat16 [3, 2, 12288, 384], P(None, None, 'seg'), may hold values from -0.21875 to 0.21875
- projection: bfloat16 [2, 6144, 384], P(None, 'seg'), may hold values from -0.21875 to 0.21875
- transfers: bfloat16 [5, 2, 6144, 192], P(None, None, 'seg'), may hold values from -0.3125 to 0.3125
- interpolation: bfloat16 [2, 12288, 192], P(None, 'seg'), may hold values from -0.3125 to 0.3125
- precondition: float32 [2, 12288], P(None, 'seg'), may hold values from 0.5 to 1.5
Outputs:
- result: float32 [2, 12288, 256], P(None, 'seg')
All inputs are finite; a program needn't handle non-finite values.
Results may differ from a plain program's by a relative error of at most 0.007.
Values may be sent and summed in bfloat16 or wider, within the bound.
A program may use at most 64 MiB of HBM per device.

v0:
```python
import functools

import jax
import jax.numpy as jnp
from jax import lax
from jax.experimental import pallas as pl
from jax.experimental.pallas import tpu as pltpu
from jax.sharding import PartitionSpec as P

MESH = pl.DeviceIdType.MESH
BF16 = jnp.bfloat16
F32 = jnp.float32


def turned(packed):
    width = packed.shape[-1] // 2
    return jnp.concatenate([-packed[:, width:], packed[:, :width]], axis=1)


def packed_product(real, imag, packed):
    return jnp.dot(real, packed, preferred_element_type=F32) + jnp.dot(
        imag, turned(packed), preferred_element_type=F32
    )


def kernel(
    devices,
    levels,
    chunks,
    pieces,
    density_hbm,
    near_hbm,
    projection_hbm,
    transfers_hbm,
    interpolation_hbm,
    precondition_hbm,
    result,
    density,
    near,
    projection,
    transfers,
    interpolation_turned,
    precondition,
    interpolation,
    scale,
    own,
    chip,
    cross,
    sent,
    joined,
    acc,
    load_sem,
    halo_send,
    halo_recv,
    level_send,
    level_recv,
):
    me = lax.axis_index("seg")
    bits = [lax.rem(lax.div(me, 1 << l), 2) for l in range(levels)]
    partners = [me + (1 - 2 * bits[l]) * (1 << l) for l in range(levels)]
    outside = lax.rem(me + devices - 1 + 2 * bits[0], devices)
    neighbours = [partners[0], outside]
    neighbour_blocks = [2 - bits[0], 1 + bits[0]]
    halo = [chip, cross]
    half = projection.shape[1] // 2
    width = density.shape[2] // chunks
    piece_rows = density.shape[1] // pieces

    barrier = pltpu.get_barrier_semaphore()
    for other in partners + [outside]:
        pl.semaphore_signal(barrier, inc=1, device_id=(other,), device_id_type=MESH)

    def columns(c):
        return pl.ds(c * width, width)

    density_loads = [
        pltpu.make_async_copy(
            density_hbm.at[:, :, columns(c)], density.at[:, :, columns(c)], load_sem.at[5 + c]
        )
        for c in range(chunks)
    ]
    load_projection, load_transfers, load_near, load_interpolation, load_precondition = [
        pltpu.make_async_copy(source, target, load_sem.at[i])
        for i, (source, target) in enumerate(
            [
                (projection_hbm, projection),
                (transfers_hbm, transfers),
                (near_hbm, near),
                (interpolation_hbm, interpolation_turned),
                (precondition_hbm, precondition),
            ]
        )
    ]
    for load in density_loads:
        load.start()
    load_projection.start()

    def to_neighbour(way, c, piece):
        rows = pl.ds(piece * piece_rows, piece_rows)
        copy = pltpu.make_async_remote_copy(
            src_ref=own.at[c, rows],
            dst_ref=halo[way].at[c, rows],
            send_sem=halo_send.at[way, c, piece],
            recv_sem=halo_recv.at[way, c, piece],
            device_id=(neighbours[way],),
            device_id_type=MESH,
        )
        copy.start()
        halos[way][c].append(copy)

    def exchange(level, c, coeffs):
        keep = pl.ds(pl.multiple_of(bits[level] * half, half), half)
        give = pl.ds(pl.multiple_of((1 - bits[level]) * half, half), half)
        sent[level, c] = coeffs.astype(BF16)
        copy = pltpu.make_async_remote_copy(
            src_ref=sent.at[level, c, give],
            dst_ref=joined.at[level, c, keep],
            send_sem=level_send.at[level, c],
            recv_sem=level_recv.at[level, c],
            device_id=(partners[level],),
            device_id_type=MESH,
        )
        copy.start()
        joined[level, c, keep] = sent[level, c, keep]
        return copy

    def near_own(c):
        acc[c] = packed_product(near[0, 0], near[0, 1], own[c])

    def near_halo(way, c):
        for copy in halos[way][c]:
            copy.wait_recv()
        block = neighbour_blocks[way]
        acc[c] += packed_product(near[block, 0], near[block, 1], halo[way][c])

    halos = [[[] for _ in range(chunks)] for _ in range(2)]
    turns = [(c, piece) for c in range(chunks) for piece in range(pieces)]
    flying = [[None] * chunks for _ in range(levels)]
    for c in range(chunks):
        density_loads[c].wait()
        for part in range(2):
            own[c, :, part * width : (part + 1) * width] = density[
                part, :, c * width : (c + 1) * width
            ].astype(BF16)
        if c == 0:
            pl.semaphore_wait(barrier, levels + 1)
            to_neighbour(1, *turns[0])
    load_transfers.start()
    load_near.start()
    load_interpolation.start()
    load_precondition.start()
    load_projection.wait()
    for c in range(chunks):
        flying[0][c] = exchange(0, c, packed_product(projection[0], projection[1], own[c]))
    for turn in turns:
        to_neighbour(0, *turn)
    load_near.wait()
    near_own(0)
    load_transfers.wait()

    for level in range(levels):
        for c in range(chunks):
            flying[level][c].wait_recv()
            coeffs = packed_product(transfers[level, 0], transfers[level, 1], joined[level, c])
            if level + 1 < levels:
                flying[level + 1][c] = exchange(level + 1, c, coeffs)
                continue
            far = packed_product(interpolation[0], interpolation[1], coeffs.astype(BF16))
            whole = acc[c] + far
            real, imag = whole[:, :width], whole[:, width:]
            for part, value in enumerate(
                [scale[0] * real - scale[1] * imag, scale[0] * imag + scale[1] * real]
            ):
                result[part, :, c * width : (c + 1) * width] = value
        if level + 1 < levels:
            for turn in turns[level + 1 :] if level + 2 == levels else turns[level + 1 : level + 2]:
                to_neighbour(1, *turn)
        if level == 0:
            for c in range(1, chunks):
                near_own(c)
        if level == 1:
            for c in range(chunks):
                near_halo(0, c)
        if level == 2:
            load_interpolation.wait()
            load_precondition.wait()
            for part in range(2):
                interpolation[part] = interpolation_turned[part].T
                row = precondition[part : part + 1, :]
                scale[part] = jnp.broadcast_to(row, (width, row.shape[1])).T
        if level == 3:
            for c in range(chunks):
                near_halo(1, c)
    for copies in halos[0] + halos[1] + flying:
        for copy in copies:
            copy.wait_send()


def body(density, near_blocks, projection, transfers, interpolation, precondition):
    devices = lax.axis_size("seg")
    levels = transfers.shape[0]
    rows, angles = density.shape[1:]
    rank = projection.shape[1]
    chunks = 2 if angles % 256 == 0 else 1
    width = angles // chunks
    pieces = 2 if rows % 32 == 0 else 1
    hbm_spec = pl.BlockSpec(memory_space=pltpu.HBM)
    interpolation_turned = jnp.swapaxes(interpolation, 1, 2)
    return pl.pallas_call(
        functools.partial(kernel, devices, levels, chunks, pieces),
        out_shape=jax.ShapeDtypeStruct(density.shape, F32),
        in_specs=[hbm_spec] * 6,
        out_specs=pl.BlockSpec(memory_space=pltpu.VMEM),
        scratch_shapes=[
            pltpu.VMEM(density.shape, F32),
            pltpu.VMEM(near_blocks.shape, BF16),
            pltpu.VMEM(projection.shape, BF16),
            pltpu.VMEM(transfers.shape, BF16),
            pltpu.VMEM(interpolation_turned.shape, BF16),
            pltpu.VMEM(precondition.shape, F32),
            pltpu.VMEM(interpolation.shape, BF16),
            pltpu.VMEM((2, rows, width), F32),
            pltpu.VMEM((chunks, rows, 2 * width), BF16),
            pltpu.VMEM((chunks, rows, 2 * width), BF16),
            pltpu.VMEM((chunks, rows, 2 * width), BF16),
            pltpu.VMEM((levels, chunks, rank, 2 * width), BF16),
            pltpu.VMEM((levels, chunks, rank, 2 * width), BF16),
            pltpu.VMEM((chunks, rows, 2 * width), F32),
            pltpu.SemaphoreType.DMA((5 + chunks,)),
            pltpu.SemaphoreType.DMA((2, chunks, pieces)),
            pltpu.SemaphoreType.DMA((2, chunks, pieces)),
            pltpu.SemaphoreType.DMA((levels, chunks)),
            pltpu.SemaphoreType.DMA((levels, chunks)),
        ],
        compiler_params=pltpu.CompilerParams(
            collective_id=0, has_side_effects=True, vmem_limit_bytes=32 * 1024 * 1024
        ),
        name="boundary_matvec",
    )(
        *[
            pltpu.with_memory_space_constraint(array, pltpu.HBM)
            for array in (
                density,
                near_blocks,
                projection,
                transfers,
                interpolation_turned,
                precondition,
            )
        ]
    )


def solution(mesh):
    placed = (
        P(None, "seg", None),
        P(None, None, "seg", None),
        P(None, "seg", None),
        P(None, None, "seg", None),
        P(None, "seg", None),
        P(None, "seg"),
    )
    return jax.shard_map(
        body, mesh=mesh, in_specs=placed, out_specs=P(None, "seg", None), check_vma=False
    )
```

profile of v0, /device:TPU:0, one launch (start us, length us, event | category | flops | bytes accessed | tf_op | source)
XLA Modules:
  0.0 26.8 jit_solution(13967384559640922010)
XLA Ops:
  0.0 25.9 %boundary_matvec.1 = f32[2,384,256]{2,1,0:T(8,128)S(1)} custom-call(f32[2,384,256]{2,1,0:T(8,128)} %density_hbm.1, bf16[3,2,384,384]{3,2,1,0:T(8,128)(2,1)} %near_hbm.1, bf16[2,192,384]{2,1,0:T(8,128)(2,1)} %projection_hbm.1, bf16[5,2,192,192]{3,2,1,0:T(8,128)(2,1)} %transfers_hbm.1, bf16[2,192,384]{2,1,0:T(8,128)(2,1)} %bitcast.1, f32[2,384]{1,0:T(2,128)} %precondition_hbm.1), custom_call_target="tpu_custom_call" | custom-call | tf_op jit(solution)/shard_map/boundary_matvec/pallas_call | solution.py:209
  25.9 0.9 %copy.8 = f32[2,384,256]{2,1,0:T(8,128)} copy(f32[2,384,256]{2,1,0:T(8,128)S(1)} %boundary_matvec.1) | data formatting | bytes 1572864
where the time goes:
time: 27 us; the launch traced here: 26.8 us
  Pallas kernels  25.9 us (96%)
  local copies, waits for them, and re-layouts  0.88 us (3%)
    pallas_call x1, Pallas kernels, body(): pl.pallas_call(functools.partial(kernel, devices, levels, chunks, pieces)...  25.9 us
    unnamed x1, local copies, waits for them, and re-layouts  0.88 us

commit v1 on v0

--- a/solution.py
+++ b/solution.py
@@ -60,6 +60,7 @@
     partners = [me + (1 - 2 * bits[l]) * (1 << l) for l in range(levels)]
     outside = lax.rem(me + devices - 1 + 2 * bits[0], devices)
     neighbours = [partners[0], outside]
+    long_route = bits[0] == bits[1]
     neighbour_blocks = [2 - bits[0], 1 + bits[0]]
     halo = [chip, cross]
     half = projection.shape[1] // 2
@@ -105,8 +106,8 @@
             device_id=(neighbours[way],),
             device_id_type=MESH,
         )
-        copy.start()
         halos[way][c].append(copy)
+        return copy
 
     def exchange(level, c, coeffs):
         keep = pl.ds(pl.multiple_of(bits[level] * half, half), half)
@@ -135,6 +136,22 @@
 
     halos = [[[] for _ in range(chunks)] for _ in range(2)]
     turns = [(c, piece) for c in range(chunks) for piece in range(pieces)]
+    inner = [to_neighbour(0, *turn) for turn in turns]
+    outer = [to_neighbour(1, *turn) for turn in turns]
+    split = len(outer) // 2
+
+    def start_outer(first, last):
+        if first is not None:
+            @pl.when(long_route)
+            def _():
+                for copy in first:
+                    copy.start()
+        if last is not None:
+            @pl.when(jnp.logical_not(long_route))
+            def _():
+                for copy in last:
+                    copy.start()
+
     flying = [[None] * chunks for _ in range(levels)]
     for c in range(chunks):
         density_loads[c].wait()
@@ -142,9 +159,8 @@
             own[c, :, part * width : (part + 1) * width] = density[
                 part, :, c * width : (c + 1) * width
             ].astype(BF16)
-        if c == 0:
-            pl.semaphore_wait(barrier, levels + 1)
-            to_neighbour(1, *turns[0])
+    pl.semaphore_wait(barrier, levels + 1)
+    start_outer(outer[:split], None)
     load_transfers.start()
     load_near.start()
     load_interpolation.start()
@@ -152,10 +168,8 @@
     load_projection.wait()
     for c in range(chunks):
         flying[0][c] = exchange(0, c, packed_product(projection[0], projection[1], own[c]))
-    for turn in turns:
-        to_neighbour(0, *turn)
-    load_near.wait()
-    near_own(0)
+    for copy in inner:
+        copy.start()
     load_transfers.wait()
 
     for level in range(levels):
@@ -172,13 +186,13 @@
                 [scale[0] * real - scale[1] * imag, scale[0] * imag + scale[1] * real]
             ):
                 result[part, :, c * width : (c + 1) * width] = value
-        if level + 1 < levels:
-            for turn in turns[level + 1 :] if level + 2 == levels else turns[level + 1 : level + 2]:
-                to_neighbour(1, *turn)
         if level == 0:
-            for c in range(1, chunks):
+            start_outer(outer[split:], outer[:split])
+            load_near.wait()
+            for c in range(chunks):
                 near_own(c)
         if level == 1:
+            start_outer(None, outer[split:])
             for c in range(chunks):
                 near_halo(0, c)
         if level == 2:

time: 27 us -> 27.7 us (1.026)
  Pallas kernels: 25.9 us -> 26.7 us
    pallas_call x1, Pallas kernels: 25.9 us -> 26.7 us  [body(): pl.pallas_call(functools.partial(kernel, devices, levels, chunks, pieces)...]
where the time goes in v1:
time: 27.7 us; the launch traced here: 27.5 us
  Pallas kernels  26.7 us (96%)
  local copies, waits for them, and re-layouts  0.88 us (3%)
    pallas_call x1, Pallas kernels, body(): pl.pallas_call(functools.partial(kernel, devices, levels, chunks, pieces)...  26.7 us
    unnamed x1, local copies, waits for them, and re-layouts  0.88 us

profile of v1, /device:TPU:0, one launch (start us, length us, event | category | flops | bytes accessed | tf_op | source)
XLA Modules:
  0.0 27.5 jit_solution(6712075760133119400)
XLA Ops:
  0.0 26.7 %boundary_matvec.1 = f32[2,384,256]{2,1,0:T(8,128)S(1)} custom-call(f32[2,384,256]{2,1,0:T(8,128)} %density_hbm.1, bf16[3,2,384,384]{3,2,1,0:T(8,128)(2,1)} %near_hbm.1, bf16[2,192,384]{2,1,0:T(8,128)(2,1)} %projection_hbm.1, bf16[5,2,192,192]{3,2,1,0:T(8,128)(2,1)} %transfers_hbm.1, bf16[2,192,384]{2,1,0:T(8,128)(2,1)} %bitcast.1, f32[2,384]{1,0:T(2,128)} %precondition_hbm.1), custom_call_target="tpu_custom_call" | custom-call | tf_op jit(solution)/shard_map/boundary_matvec/pallas_call | solution.py:223
  26.7 0.9 %copy.8 = f32[2,384,256]{2,1,0:T(8,128)} copy(f32[2,384,256]{2,1,0:T(8,128)S(1)} %boundary_matvec.1) | data formatting | bytes 1572864

commit v2 on v0

--- a/solution.py
+++ b/solution.py
@@ -133,9 +133,34 @@
         block = neighbour_blocks[way]
         acc[c] += packed_product(near[block, 0], near[block, 1], halo[way][c])
 
+    def finish(c, coeffs):
+        far = packed_product(interpolation[0], interpolation[1], coeffs.astype(BF16))
+        whole = acc[c] + far
+        real, imag = whole[:, :width], whole[:, width:]
+        for part, value in enumerate(
+            [scale[0] * real - scale[1] * imag, scale[0] * imag + scale[1] * real]
+        ):
+            result[part, :, c * width : (c + 1) * width] = value
+
+    def prepare_tail():
+        load_interpolation.wait()
+        load_precondition.wait()
+        for part in range(2):
+            interpolation[part] = interpolation_turned[part].T
+            row = precondition[part : part + 1, :]
+            scale[part] = jnp.broadcast_to(row, (width, row.shape[1])).T
+
     halos = [[[] for _ in range(chunks)] for _ in range(2)]
     turns = [(c, piece) for c in range(chunks) for piece in range(pieces)]
     flying = [[None] * chunks for _ in range(levels)]
+    spare = [functools.partial(near_own, c) for c in range(chunks)]
+    spare += [functools.partial(near_halo, 0, c) for c in range(chunks)]
+    spare.append(prepare_tail)
+
+    def one_spare():
+        if spare:
+            spare.pop(0)()
+
     for c in range(chunks):
         density_loads[c].wait()
         for part in range(2):
@@ -143,52 +168,37 @@
                 part, :, c * width : (c + 1) * width
             ].astype(BF16)
         if c == 0:
+            load_transfers.start()
+            load_near.start()
+            load_interpolation.start()
+            load_precondition.start()
+            load_projection.wait()
             pl.semaphore_wait(barrier, levels + 1)
+        flying[0][c] = exchange(0, c, packed_product(projection[0], projection[1], own[c]))
+        if c == 0:
             to_neighbour(1, *turns[0])
-    load_transfers.start()
-    load_near.start()
-    load_interpolation.start()
-    load_precondition.start()
-    load_projection.wait()
-    for c in range(chunks):
-        flying[0][c] = exchange(0, c, packed_product(projection[0], projection[1], own[c]))
     for turn in turns:
         to_neighbour(0, *turn)
-    load_near.wait()
-    near_own(0)
     load_transfers.wait()
 
     for level in range(levels):
         for c in range(chunks):
             flying[level][c].wait_recv()
             coeffs = packed_product(transfers[level, 0], transfers[level, 1], joined[level, c])
-            if level + 1 < levels:
-                flying[level + 1][c] = exchange(level + 1, c, coeffs)
+            if level + 1 == levels:
+                finish(c, coeffs)
                 continue
-            far = packed_product(interpolation[0], interpolation[1], coeffs.astype(BF16))
-            whole = acc[c] + far
-            real, imag = whole[:, :width], whole[:, width:]
-            for part, value in enumerate(
-                [scale[0] * real - scale[1] * imag, scale[0] * imag + scale[1] * real]
-            ):
-                result[part, :, c * width : (c + 1) * width] = value
+            flying[level + 1][c] = exchange(level + 1, c, coeffs)
+            if c == 0:
+                if level == 0:
+                    load_near.wait()
+                one_spare()
         if level + 1 < levels:
             for turn in turns[level + 1 :] if level + 2 == levels else turns[level + 1 : level + 2]:
                 to_neighbour(1, *turn)
-        if level == 0:
-            for c in range(1, chunks):
-                near_own(c)
-        if level == 1:
-            for c in range(chunks):
-                near_halo(0, c)
-        if level == 2:
-            load_interpolation.wait()
-            load_precondition.wait()
-            for part in range(2):
-                interpolation[part] = interpolation_turned[part].T
-                row = precondition[part : part + 1, :]
-                scale[part] = jnp.broadcast_to(row, (width, row.shape[1])).T
-        if level == 3:
+        if level + 2 == levels:
+            while spare:
+                one_spare()
             for c in range(chunks):
                 near_halo(1, c)
     for copies in halos[0] + halos[1] + flying:

time: 27 us -> 26.3 us (0.974)
  Pallas kernels: 25.9 us -> 25.3 us
    pallas_call x1, Pallas kernels: 25.9 us -> 25.3 us  [body(): pl.pallas_call(functools.partial(kernel, devices, levels, chunks, pieces)...]
where the time goes in v2:
time: 26.3 us; the launch traced here: 26.2 us
  Pallas kernels  25.3 us (96%)
  local copies, waits for them, and re-layouts  0.88 us (3%)
    pallas_call x1, Pallas kernels, body(): pl.pallas_call(functools.partial(kernel, devices, levels, chunks, pieces)...  25.3 us
    unnamed x1, local copies, waits for them, and re-layouts  0.88 us

profile of v2, /device:TPU:0, one launch (start us, length us, event | category | flops | bytes accessed | tf_op | source)
XLA Modules:
  0.0 26.2 jit_solution(16761140420747301987)
XLA Ops:
  0.0 25.3 %boundary_matvec.1 = f32[2,384,256]{2,1,0:T(8,128)S(1)} custom-call(f32[2,384,256]{2,1,0:T(8,128)} %density_hbm.1, bf16[3,2,384,384]{3,2,1,0:T(8,128)(2,1)} %near_hbm.1, bf16[2,192,384]{2,1,0:T(8,128)(2,1)} %projection_hbm.1, bf16[5,2,192,192]{3,2,1,0:T(8,128)(2,1)} %transfers_hbm.1, bf16[2,192,384]{2,1,0:T(8,128)(2,1)} %bitcast.1, f32[2,384]{1,0:T(2,128)} %precondition_hbm.1), custom_call_target="tpu_custom_call" | custom-call | tf_op jit(solution)/shard_map/boundary_matvec/pallas_call | solution.py:219
  25.3 0.9 %copy.8 = f32[2,384,256]{2,1,0:T(8,128)} copy(f32[2,384,256]{2,1,0:T(8,128)S(1)} %boundary_matvec.1) | data formatting | bytes 1572864

commit v3 on v2

--- a/solution.py
+++ b/solution.py
@@ -60,6 +60,10 @@
     partners = [me + (1 - 2 * bits[l]) * (1 << l) for l in range(levels)]
     outside = lax.rem(me + devices - 1 + 2 * bits[0], devices)
     neighbours = [partners[0], outside]
+    same_plane = bits[1] != bits[2]
+    longest = jnp.logical_and(bits[1] == bits[2], bits[0] == bits[1])
+    beside = jnp.logical_and(bits[1] == bits[2], bits[0] != bits[1])
+    routes = [longest, beside, same_plane]
     neighbour_blocks = [2 - bits[0], 1 + bits[0]]
     halo = [chip, cross]
     half = projection.shape[1] // 2
@@ -105,8 +109,8 @@
             device_id=(neighbours[way],),
             device_id_type=MESH,
         )
-        copy.start()
         halos[way][c].append(copy)
+        return copy
 
     def exchange(level, c, coeffs):
         keep = pl.ds(pl.multiple_of(bits[level] * half, half), half)
@@ -152,6 +156,17 @@
 
     halos = [[[] for _ in range(chunks)] for _ in range(2)]
     turns = [(c, piece) for c in range(chunks) for piece in range(pieces)]
+    inner = [to_neighbour(0, *turn) for turn in turns]
+    outer = [to_neighbour(1, *turn) for turn in turns]
+
+    def start_outer(*runs):
+        for route, run in zip(routes, runs):
+            if run:
+                @pl.when(route)
+                def _():
+                    for i in run:
+                        outer[i].start()
+
     flying = [[None] * chunks for _ in range(levels)]
     spare = [functools.partial(near_own, c) for c in range(chunks)]
     spare += [functools.partial(near_halo, 0, c) for c in range(chunks)]
@@ -176,9 +191,10 @@
             pl.semaphore_wait(barrier, levels + 1)
         flying[0][c] = exchange(0, c, packed_product(projection[0], projection[1], own[c]))
         if c == 0:
-            to_neighbour(1, *turns[0])
-    for turn in turns:
-        to_neighbour(0, *turn)
+            start_outer([0, 1], [], [0])
+    start_outer([2], [], [])
+    for copy in inner:
+        copy.start()
     load_transfers.wait()
 
     for level in range(levels):
@@ -193,9 +209,12 @@
                 if level == 0:
                     load_near.wait()
                 one_spare()
-        if level + 1 < levels:
-            for turn in turns[level + 1 :] if level + 2 == levels else turns[level + 1 : level + 2]:
-                to_neighbour(1, *turn)
+        if level == 0:
+            start_outer([3], [0], [1])
+        if level == 1:
+            start_outer([], [1, 2], [2])
+        if level == 2:
+            start_outer([], [3], [3])
         if level + 2 == levels:
             while spare:
                 one_spare()
@@ -211,9 +230,9 @@
     levels = transfers.shape[0]
     rows, angles = density.shape[1:]
     rank = projection.shape[1]
-    chunks = 2 if angles % 256 == 0 else 1
+    chunks = 2
     width = angles // chunks
-    pieces = 2 if rows % 32 == 0 else 1
+    pieces = 2
     hbm_spec = pl.BlockSpec(memory_space=pltpu.HBM)
     interpolation_turned = jnp.swapaxes(interpolation, 1, 2)
     return pl.pallas_call(

time: 26.3 us -> 28.1 us (1.068)
  Pallas kernels: 25.3 us -> 27 us
    pallas_call x1, Pallas kernels: 25.3 us -> 27 us  [body(): pl.pallas_call(functools.partial(kernel, devices, levels, chunks, pieces)...]
where the time goes in v3:
time: 28.1 us; the launch traced here: 27.9 us
  Pallas kernels  27 us (96%)
  local copies, waits for them, and re-layouts  0.88 us (3%)
    pallas_call x1, Pallas kernels, body(): pl.pallas_call(functools.partial(kernel, devices, levels, chunks, pieces)...  27 us
    unnamed x1, local copies, waits for them, and re-layouts  0.88 us

profile of v3, /device:TPU:0, one launch (start us, length us, event | category | flops | bytes accessed | tf_op | source)
XLA Modules:
  0.0 27.9 jit_solution(9836302320689483869)
XLA Ops:
  0.0 27.0 %boundary_matvec.1 = f32[2,384,256]{2,1,0:T(8,128)S(1)} custom-call(f32[2,384,256]{2,1,0:T(8,128)} %density_hbm.1, bf16[3,2,384,384]{3,2,1,0:T(8,128)(2,1)} %near_hbm.1, bf16[2,192,384]{2,1,0:T(8,128)(2,1)} %projection_hbm.1, bf16[5,2,192,192]{3,2,1,0:T(8,128)(2,1)} %transfers_hbm.1, bf16[2,192,384]{2,1,0:T(8,128)(2,1)} %bitcast.1, f32[2,384]{1,0:T(2,128)} %precondition_hbm.1), custom_call_target="tpu_custom_call" | custom-call | tf_op jit(solution)/shard_map/boundary_matvec/pallas_call | solution.py:238
  27.0 0.9 %copy.8 = f32[2,384,256]{2,1,0:T(8,128)} copy(f32[2,384,256]{2,1,0:T(8,128)S(1)} %boundary_matvec.1) | data formatting | bytes 1572864

commit v4 on v2

--- a/solution.py
+++ b/solution.py
@@ -183,6 +183,8 @@
 
     for level in range(levels):
         for c in range(chunks):
+            if level + 1 == levels:
+                near_halo(1, c)
             flying[level][c].wait_recv()
             coeffs = packed_product(transfers[level, 0], transfers[level, 1], joined[level, c])
             if level + 1 == levels:
@@ -199,8 +201,6 @@
         if level + 2 == levels:
             while spare:
                 one_spare()
-            for c in range(chunks):
-                near_halo(1, c)
     for copies in halos[0] + halos[1] + flying:
         for copy in copies:
             copy.wait_send()

time: 26.3 us -> 26.3 us (level)
  no operation moved by 1% of the time
where the time goes in v4:
time: 26.3 us; the launch traced here: 26.2 us
  Pallas kernels  25.3 us (96%)
  local copies, waits for them, and re-layouts  0.88 us (3%)
    pallas_call x1, Pallas kernels, body(): pl.pallas_call(functools.partial(kernel, devices, levels, chunks, pieces)...  25.3 us
    unnamed x1, local copies, waits for them, and re-layouts  0.88 us

profile of v4, /device:TPU:0, one launch (start us, length us, event | category | flops | bytes accessed | tf_op | source)
XLA Modules:
  0.0 26.2 jit_solution(13797880074040436182)
XLA Ops:
  0.0 25.3 %boundary_matvec.1 = f32[2,384,256]{2,1,0:T(8,128)S(1)} custom-call(f32[2,384,256]{2,1,0:T(8,128)} %density_hbm.1, bf16[3,2,384,384]{3,2,1,0:T(8,128)(2,1)} %near_hbm.1, bf16[2,192,384]{2,1,0:T(8,128)(2,1)} %projection_hbm.1, bf16[5,2,192,192]{3,2,1,0:T(8,128)(2,1)} %transfers_hbm.1, bf16[2,192,384]{2,1,0:T(8,128)(2,1)} %bitcast.1, f32[2,384]{1,0:T(2,128)} %precondition_hbm.1), custom_call_target="tpu_custom_call" | custom-call | tf_op jit(solution)/shard_map/boundary_matvec/pallas_call | solution.py:219
  25.3 0.9 %copy.8 = f32[2,384,256]{2,1,0:T(8,128)} copy(f32[2,384,256]{2,1,0:T(8,128)S(1)} %boundary_matvec.1) | data formatting | bytes 1572864
